TPU v7x, 32 devices: a whole 2x2x4 slice. The times are simulated.
32 devices in a mesh: dp: 4 (over z), fsdp: 4 (over y, core), enc: 2 (over x).
Axes of the slice: x: 2, y: 2, z: 4, core: 2. Of those that a mesh axis runs over, the one named last changes fastest.
Arguments:
- queries: bfloat16 [3072, 4096], P(('dp', 'fsdp'), 'enc'), may hold values from -9 to 9
- nbr_keys: bfloat16 [96, 128, 4096], P('dp', 'fsdp', 'enc'), may hold values from -6 to 6
- nbr_values: bfloat16 [96, 128, 4096], P('dp', 'fsdp', 'enc'), may hold values from -6 to 6
- out_proj: bfloat16 [4096, 8192], P('enc', 'fsdp'), may hold values from -0.09375 to 0.09375
- nbr_source: int32 [48, 2], replicated, may hold values from 0 to 3, as said below
- nbr_index: int32 [48, 2], replicated, may hold values from 0 to 23
- nbr_count: int32 [48], replicated, may hold values from 1 to 2
- cotangent: bfloat16 [3072, 8192], P('dp', 'fsdp'), may hold values from -2.390625 to 2.390625
Outputs:
- attended: bfloat16 [3072, 4096], P(('dp', 'fsdp'), 'enc')
- grad_queries: bfloat16 [3072, 4096], P(('dp', 'fsdp'), 'enc')
- grad_keys: bfloat16 [96, 128, 4096], P('dp', 'fsdp', 'enc')
- grad_values: bfloat16 [96, 128, 4096], P('dp', 'fsdp', 'enc')
- grad_proj: bfloat16 [4096, 8192], P('enc', 'fsdp')
Inputs may be any that keep to these rules, and one draw needn't show every extreme that they name: `nbr_source`: among the 6 slots of the spans of one device, no source group is named more than 2 times, and some group exactly 2 times.
All inputs are finite; a program needn't handle non-finite values.
Results may differ from a plain program's by a relative error of at most 0.013.
Values may be sent and summed in bfloat16 or wider, within the bound.
No kernel may reach another device: no remote copies, remote signals or barrier semaphores. Data moves between devices by JAX's collectives and lax.ppermute only.
A program may use at most 128 MiB of HBM per device.

v0:
```python
import math

import jax
import jax.numpy as jnp
from jax import lax
from jax.sharding import PartitionSpec as P

HEAD_DIM = 128
SPAN = 64
SLOTS = 2


def local(queries, nbr_keys, nbr_values, out_proj, nbr_source, nbr_index, nbr_count, cotangent):
    dp_count = lax.axis_size("dp")
    fsdp_count = lax.axis_size("fsdp")
    peer_count = dp_count * fsdp_count
    token_rows, width_halved = queries.shape
    heads_here = width_halved // HEAD_DIM
    spans_here = token_rows // SPAN
    slot_count = SLOTS * spans_here
    capacity = (slot_count + dp_count - 1) // dp_count
    group_size, piece_rows, piece_width = nbr_keys.shape
    neighbour_len = piece_rows * fsdp_count
    scale = 1.0 / math.sqrt(HEAD_DIM)
    my_group = lax.axis_index("dp")
    my_place = my_group * fsdp_count + lax.axis_index("fsdp")
    all_sources = nbr_source.reshape(peer_count, slot_count)
    all_indices = nbr_index.reshape(peer_count, slot_count)
    slot_iota = jnp.arange(slot_count, dtype=jnp.int32)
    earlier = slot_iota[None, :] < slot_iota[:, None]
    same_source = all_sources[:, :, None] == all_sources[:, None, :]
    ranks = jnp.sum(jnp.logical_and(same_source, earlier[None]), axis=2)
    cap_iota = jnp.arange(capacity, dtype=jnp.int32)
    selected = jnp.logical_and(
        (all_sources == my_group)[:, :, None], ranks[:, :, None] == cap_iota[None, None, :]
    )
    picked = jnp.sum(jnp.where(selected, all_indices[:, :, None], 0), axis=1)
    present = jnp.any(selected, axis=1)
    flat_pick = picked.reshape(-1)
    send_keys = jnp.take(nbr_keys, flat_pick, axis=0)
    send_values = jnp.take(nbr_values, flat_pick, axis=0)
    got_keys, got_values = (
        lax.all_to_all(send_keys, ("dp", "fsdp"), split_axis=0, concat_axis=0, tiled=True),
        lax.all_to_all(send_values, ("dp", "fsdp"), split_axis=0, concat_axis=0, tiled=True),
    )
    got_keys = got_keys.reshape(dp_count, fsdp_count, capacity, piece_rows, piece_width)
    got_values = got_values.reshape(dp_count, fsdp_count, capacity, piece_rows, piece_width)
    my_sources = lax.dynamic_index_in_dim(all_sources, my_place, 0, keepdims=False)
    my_ranks = lax.dynamic_index_in_dim(ranks, my_place, 0, keepdims=False)
    slot_keys = got_keys[my_sources, :, my_ranks].reshape(
        spans_here, SLOTS * neighbour_len, heads_here, HEAD_DIM
    )
    slot_values = got_values[my_sources, :, my_ranks].reshape(
        spans_here, SLOTS * neighbour_len, heads_here, HEAD_DIM
    )
    local_counts = lax.dynamic_slice_in_dim(nbr_count, my_place * spans_here, spans_here)
    live_keys = jnp.repeat(
        jnp.arange(SLOTS)[None, :] < local_counts[:, None], neighbour_len, axis=1
    )
    query_blocks = queries.reshape(spans_here, SPAN, heads_here, HEAD_DIM)
    scores = (
        jnp.einsum("cqhd,ckhd->chqk", query_blocks, slot_keys, preferred_element_type=jnp.float32)
        * scale
    )
    scores = jnp.where(live_keys[:, None, None, :], scores, -1e30)
    peak = jnp.max(scores, axis=-1, keepdims=True)
    expo = jnp.exp(scores - peak)
    probs = expo / jnp.sum(expo, axis=-1, keepdims=True)
    probs_b = probs.astype(jnp.bfloat16)
    attended = jnp.einsum(
        "chqk,ckhd->cqhd", probs_b, slot_values, preferred_element_type=jnp.float32
    )
    attended = attended.astype(jnp.bfloat16).reshape(token_rows, width_halved)
    gathered = lax.all_gather(attended, "fsdp", axis=0, tiled=True)
    upstream = lax.psum_scatter(
        lax.dot_general(
            cotangent, out_proj, (((1,), (1,)), ((), ())), preferred_element_type=jnp.float32
        ),
        "fsdp",
        scatter_dimension=0,
        tiled=True,
    ).astype(jnp.bfloat16)
    proj_term = lax.dot_general(
        gathered, cotangent, (((0,), (0,)), ((), ())), preferred_element_type=jnp.float32
    )
    grad_proj = lax.psum(proj_term.astype(jnp.bfloat16), "dp")
    upstream_blocks = upstream.reshape(spans_here, SPAN, heads_here, HEAD_DIM)
    probability_gradient = jnp.einsum(
        "cqhd,ckhd->chqk", upstream_blocks, slot_values, preferred_element_type=jnp.float32
    )
    centre = jnp.sum(probs * probability_gradient, axis=-1, keepdims=True)
    dscores = (probs * (probability_gradient - centre) * scale).astype(jnp.bfloat16)
    grad_queries = jnp.einsum(
        "chqk,ckhd->cqhd", dscores, slot_keys, preferred_element_type=jnp.float32
    )
    grad_queries = grad_queries.astype(jnp.bfloat16).reshape(token_rows, width_halved)
    slot_key_grads = jnp.einsum(
        "chqk,cqhd->ckhd", dscores, query_blocks, preferred_element_type=jnp.float32
    ).astype(jnp.bfloat16)
    value_slot_gradients = jnp.einsum(
        "chqk,cqhd->ckhd", probs_b, upstream_blocks, preferred_element_type=jnp.float32
    ).astype(jnp.bfloat16)
    location_table = jnp.logical_and(
        my_sources[None, None, :] == jnp.arange(dp_count, dtype=jnp.int32)[:, None, None],
        my_ranks[None, None, :] == cap_iota[None, :, None],
    ).astype(jnp.bfloat16)
    key_slot_table = slot_key_grads.reshape(slot_count, fsdp_count, piece_rows * piece_width)
    value_slot_table = value_slot_gradients.reshape(
        slot_count, fsdp_count, piece_rows * piece_width
    )
    back_keys = jnp.einsum(
        "vnt,tqg->vqng", location_table, key_slot_table, preferred_element_type=jnp.float32
    ).astype(jnp.bfloat16)
    back_values = jnp.einsum(
        "vnt,tqg->vqng", location_table, value_slot_table, preferred_element_type=jnp.float32
    ).astype(jnp.bfloat16)
    ret_keys, ret_values = (
        lax.all_to_all(
            back_keys.reshape(peer_count * capacity, piece_rows, piece_width),
            ("dp", "fsdp"),
            split_axis=0,
            concat_axis=0,
            tiled=True,
        ),
        lax.all_to_all(
            back_values.reshape(peer_count * capacity, piece_rows, piece_width),
            ("dp", "fsdp"),
            split_axis=0,
            concat_axis=0,
            tiled=True,
        ),
    )
    owner_table = jnp.logical_and(
        flat_pick[None, :] == jnp.arange(group_size, dtype=jnp.int32)[:, None],
        present.reshape(-1)[None, :],
    ).astype(jnp.bfloat16)
    grad_keys = jnp.dot(
        owner_table,
        ret_keys.reshape(peer_count * capacity, piece_rows * piece_width),
        preferred_element_type=jnp.float32,
    )
    grad_values = jnp.dot(
        owner_table,
        ret_values.reshape(peer_count * capacity, piece_rows * piece_width),
        preferred_element_type=jnp.float32,
    )
    grad_keys = grad_keys.astype(jnp.bfloat16).reshape(group_size, piece_rows, piece_width)
    grad_values = grad_values.astype(jnp.bfloat16).reshape(group_size, piece_rows, piece_width)
    return (attended, grad_queries, grad_keys, grad_values, grad_proj)


def solution(mesh):
    placed = (
        P(("dp", "fsdp"), "enc"),
        P("dp", "fsdp", "enc"),
        P("dp", "fsdp", "enc"),
        P("enc", "fsdp"),
        P(),
        P(),
        P(),
        P("dp", "fsdp"),
    )
    return jax.shard_map(
        local,
        mesh=mesh,
        in_specs=placed,
        out_specs=(
            P(("dp", "fsdp"), "enc"),
            P(("dp", "fsdp"), "enc"),
            P("dp", "fsdp", "enc"),
            P("dp", "fsdp", "enc"),
            P("enc", "fsdp"),
        ),
        check_vma=False,
    )
```

profile of v0, /device:TPU:0, one launch (start us, length us, event | category | flops | bytes accessed | tf_op | source)
XLA Modules:
  0.0 762.2 jit_solution(3939653753774361601)
XLA Ops:
  7.2 0.9 copy.62
  8.1 0.1 reshape.205
  8.2 0.1 copy.64
  8.3 0.1 copy.63
  8.4 0.8 copy.66
  9.2 0.1 copy.67
  9.3 0.1 convert_reduce_fusion
  9.4 0.1 copy.69
  9.5 0.1 reshape.206
  9.6 4.7 gather_fusion.2
  14.3 4.7 gather_fusion.3
  19.0 5.8 broadcast_select_fusion
  24.9 7.4 all-to-all-start.1
  32.4 10.8 %fusion.83 = f32[768,2048]{1,0:T(8,128)} fusion(bf16[768,2048]{1,0:T(8,128)(2,1)S(1)} %copy-done, bf16[2048,2048]{1,0:T(8,128)(2,1)} %param.13), kind=kOutput, calls=%fused_computation.100 | convolution fusion | flops 6442450944 | bytes 17825792 | tf_op jit(solution)/shard_map/dot_general | solution.py:76
  43.2 67.0 %all-to-all-done.1 = bf16[32,32,2048]{2,1,0:T(8,128)(2,1)} async-done(((bf16[32,32,2048]{2,1,0:T(8,128)(2,1)}), bf16[32,32,2048]{2,1,0:T(8,128)(2,1)}, u32[]{:S(2)}, u32[]{:S(2)}) %all-to-all-start.1) | async-done | bytes 4194336 | tf_op jit(solution)/shard_map/all_to_all | solution.py:43
  110.2 19.7 %all-to-all-start = ((bf16[32,32,2048]{2,1,0:T(8,128)(2,1)}), bf16[32,32,2048]{2,1,0:T(8,128)(2,1)}, u32[]{:S(2)}, u32[]{:S(2)}) async-start(bf16[32,32,2048]{2,1,0:T(8,128)(2,1)} %get-tuple-element.7), calls=%async_computation | async-start | bytes 8388608 | tf_op jit(solution)/shard_map/all_to_all | solution.py:44
  129.9 0.2 dynamic-slice_reduce_fusion
  130.1 2.2 copy.95
  132.4 0.1 broadcast_bitcast_fusion
  132.5 4.7 gather_fusion.1
  137.1 4.7 copy.94
  141.8 65.7 %all-to-all-done = bf16[32,32,2048]{2,1,0:T(8,128)(2,1)} async-done(((bf16[32,32,2048]{2,1,0:T(8,128)(2,1)}), bf16[32,32,2048]{2,1,0:T(8,128)(2,1)}, u32[]{:S(2)}, u32[]{:S(2)}) %all-to-all-start) | async-done | bytes 4194336 | tf_op jit(solution)/shard_map/all_to_all | solution.py:44
  207.5 4.7 gather_fusion
  212.2 4.7 copy.96
  217.0 1.2 fusion.15
  218.2 2.6 fusion.82
  220.8 1.7 convert_bitcast_fusion.2
  222.5 0.2 copy.98
  222.6 0.9 copy-done.3
  223.5 2.7 convert_bitcast_fusion
  226.2 4.9 copy.84
  231.1 5.9 reshape.219
  237.0 6.7 fusion.3
  243.7 8.4 %copy.86 = bf16[4,4,2,65536]{3,2,1,0:T(2,128)(2,1)} copy(bf16[4,4,2,65536]{3,0,2,1:T(4,128)(2,1)} %fusion.3) | data formatting | bytes 8388608 | tf_op jit(solution)/shard_map/convert_element_type | solution.py:116
  252.1 11.5 %reshape.220 = bf16[32,32,2048]{2,1,0:T(8,128)(2,1)} reshape(bf16[4,4,2,65536]{3,2,1,0:T(2,128)(2,1)} %copy.86) | data formatting | bytes 8388608 | tf_op jit(solution)/shard_map/reshape | solution.py:126
  263.6 19.7 %all-to-all-start.3 = ((bf16[32,32,2048]{2,1,0:T(8,128)(2,1)}), bf16[32,32,2048]{2,1,0:T(8,128)(2,1)}, u32[]{:S(2)}, u32[]{:S(2)}) async-start(bf16[32,32,2048]{2,1,0:T(8,128)(2,1)} %reshape.220), calls=%async_computation.4 | async-start | bytes 8388608 | tf_op jit(solution)/shard_map/all_to_all | solution.py:125
  283.3 4.0 fusion.38
  287.3 0.5 copy.73
  287.8 1.1 copy.135
  288.9 0.4 all-reduce.2.cloned.1.call-start
  289.4 5.1 fusion.9
  294.5 25.7 %convert_bitcast_fusion.1 = bf16[3,256,16,128]{3,1,2,0:T(8,128)(2,1)} fusion(f32[3,16,64,256]{3,2,1,0:T(8,128)} %fusion.9, bf16[3,64,16,128]{3,2,1,0:T(8,128)(2,1)} %bitcast.103, f32[3,16,64,256]{3,2,1,0:T(8,128)} %get-tuple-element.9, f32[3,16,64]{2,1,0:T(8,128)S(1)} %get-tuple-element.8), kind=kOutput, calls=%fused_computation.22 | convolution fusion | flops 208407808 | bytes 10235904 | tf_op jit(solution)/shard_map/chqk,cqhd->ckhd/dot_general | solution.py:97
  320.2 5.6 copy.80
  325.8 5.8 reshape.215
  331.7 6.8 all-gather.2.cloned.1.call-done
  338.5 10.9 %convolution_convert_fusion.4 = bf16[2048,2048]{1,0:T(8,128)(2,1)} fusion(bf16[768,2048]{1,0:T(8,128)(2,1)} %all-gather.2.cloned.1.call-done, bf16[768,2048]{1,0:T(8,128)(2,1)S(1)} %copy-done), kind=kOutput, calls=%fused_computation.12 | convolution fusion | flops 6446645248 | bytes 14680064 | tf_op jit(solution)/shard_map/dot_general | solution.py:83
  349.4 6.8 fusion.2
  356.2 8.5 %copy.82 = bf16[4,4,2,65536]{3,2,1,0:T(2,128)(2,1)} copy(bf16[4,4,2,65536]{3,0,2,1:T(4,128)(2,1)} %fusion.2) | data formatting | bytes 8388608 | tf_op jit(solution)/shard_map/convert_element_type | solution.py:113
  364.6 11.5 %reshape.216 = bf16[32,32,2048]{2,1,0:T(8,128)(2,1)} reshape(bf16[4,4,2,65536]{3,2,1,0:T(2,128)(2,1)} %copy.82) | data formatting | bytes 8388608 | tf_op jit(solution)/shard_map/reshape | solution.py:119
  376.1 52.9 %all-to-all-start.2 = ((bf16[32,32,2048]{2,1,0:T(8,128)(2,1)}), bf16[32,32,2048]{2,1,0:T(8,128)(2,1)}, u32[]{:S(2)}, u32[]{:S(2)}) async-start(bf16[32,32,2048]{2,1,0:T(8,128)(2,1)} %reshape.216), calls=%async_computation.3 | async-start | bytes 8388608 | tf_op jit(solution)/shard_map/all_to_all | solution.py:118
  429.1 0.1 copy.78
  429.2 0.1 and.49
  429.3 23.4 %fusion.41 = bf16[3,64,16,128]{3,1,2,0:T(8,128)(2,1)} fusion(bf16[3,256,16,128]{3,2,1,0:T(8,128)(2,1)} %bitcast.97, f32[3,16,64,256]{3,2,1,0:T(8,128)} %fusion.9, f32[3,16,64,256]{3,2,1,0:T(8,128)} %get-tuple-element.9, f32[3,16,64]{2,1,0:T(8,128)S(1)} %get-tuple-element.8), kind=kOutput, calls=%fused_computation.44 | convolution fusion | flops 207228160 | bytes 10235904 | tf_op jit(solution)/shard_map/chqk,ckhd->cqhd/dot_general | solution.py:93
  452.7 1.6 copy.77
  454.4 1.1 copy.134
  455.4 4.5 copy.102
  459.9 1.0 convolution_convert_fusion.2
  460.9 3.4 copy.103
  464.3 101.7 %all-to-all-done.2 = bf16[32,32,2048]{2,1,0:T(8,128)(2,1)} async-done(((bf16[32,32,2048]{2,1,0:T(8,128)(2,1)}), bf16[32,32,2048]{2,1,0:T(8,128)(2,1)}, u32[]{:S(2)}, u32[]{:S(2)}) %all-to-all-start.2) | async-done | bytes 4194336 | tf_op jit(solution)/shard_map/all_to_all | solution.py:118
  566.0 4.8 copy.100
  570.8 1.0 convolution_convert_fusion.3
  571.8 3.4 copy.101
  575.2 171.6 %all-reduce.2.cloned.1.call-done = bf16[2048,2048]{1,0:T(8,128)(2,1)} async-done(((bf16[2048,2048]{1,0:T(8,128)(2,1)}), bf16[2048,2048]{1,0:T(8,128)(2,1)}) %all-reduce.2.cloned.1.call-update) | async-done | bytes 8388624 | tf_op jit(solution)/shard_map/psum | solution.py:86
  746.8 8.4 %copy.137 = bf16[2048,2048]{1,0:T(8,128)(2,1)} copy(bf16[2048,2048]{1,0:T(8,128)(2,1)} %all-reduce.2.cloned.1.call-done) | data formatting | bytes 16777216
  (32 shorter events, 0.4 us)
Async XLA Ops:
  7.2 25.2 %copy-start = (bf16[768,2048]{1,0:T(8,128)(2,1)S(1)}, bf16[768,2048]{1,0:T(8,128)(2,1)}, u32[]{:S(2)}) copy-start(bf16[768,2048]{1,0:T(8,128)(2,1)} %param.17) | copy-start | bytes 9437188
  24.9 85.3 %all-to-all-start.1 = ((bf16[32,32,2048]{2,1,0:T(8,128)(2,1)}), bf16[32,32,2048]{2,1,0:T(8,128)(2,1)}, u32[]{:S(2)}, u32[]{:S(2)}) async-start(bf16[32,32,2048]{2,1,0:T(8,128)(2,1)} %get-tuple-element.6), calls=%async_computation.1 | async-start | bytes 8388608 | tf_op jit(solution)/shard_map/all_to_all | solution.py:43
  32.3 188.4 %reduce-scatter.2.cloned.1.call-start = ((), (), s32[]{:S(2)}) async-start(), calls=%async_computation.5 | async-start | bytes 7864320 | tf_op jit(solution)/shard_map/reduce_scatter | solution.py:75
  110.2 22.1 %copy-start.4 = (s32[48]{0:T(128)S(1)}, s32[48]{0:T(128)}, u32[]{:S(2)}) copy-start(s32[48]{0:T(128)} %param.16) | copy-start | bytes 580
  110.2 97.4 %all-to-all-start = ((bf16[32,32,2048]{2,1,0:T(8,128)(2,1)}), bf16[32,32,2048]{2,1,0:T(8,128)(2,1)}, u32[]{:S(2)}, u32[]{:S(2)}) async-start(bf16[32,32,2048]{2,1,0:T(8,128)(2,1)} %get-tuple-element.7), calls=%async_computation | async-start | bytes 8388608 | tf_op jit(solution)/shard_map/all_to_all | solution.py:44
  212.2 4.7 copy-start.1
  212.2 4.7 copy-start.2
  220.8 2.8 copy-start.5
  222.6 0.9 copy-start.3
  263.6 112.5 %all-to-all-start.3 = ((bf16[32,32,2048]{2,1,0:T(8,128)(2,1)}), bf16[32,32,2048]{2,1,0:T(8,128)(2,1)}, u32[]{:S(2)}, u32[]{:S(2)}) async-start(bf16[32,32,2048]{2,1,0:T(8,128)(2,1)} %reshape.220), calls=%async_computation.4 | async-start | bytes 8388608 | tf_op jit(solution)/shard_map/all_to_all | solution.py:125
  283.3 55.2 %all-gather.2.cloned.1.call-start = ((), (), s32[]{:S(2)}) async-start(), calls=%async_computation.6 | async-start | bytes 3932160 | tf_op jit(solution)/shard_map/all_gather | solution.py:74
  288.9 457.8 %all-reduce.2.cloned.1.call-start = ((), (), s32[]{:S(2)}) async-start(), calls=%async_computation.7 | async-start | bytes 16777216 | tf_op jit(solution)/shard_map/psum | solution.py:86
  376.1 189.9 %all-to-all-start.2 = ((bf16[32,32,2048]{2,1,0:T(8,128)(2,1)}), bf16[32,32,2048]{2,1,0:T(8,128)(2,1)}, u32[]{:S(2)}, u32[]{:S(2)}) async-start(bf16[32,32,2048]{2,1,0:T(8,128)(2,1)} %reshape.216), calls=%async_computation.3 | async-start | bytes 8388608 | tf_op jit(solution)/shard_map/all_to_all | solution.py:118
Sparse Core Ops, SparseCore 0:
  43.3 79.0 reduce-scatter.1
  289.1 49.3 all-gather.1
  349.5 397.2 all-reduce.1
where the time goes:
time: 772 us; the launch traced here: 762 us
  waiting for transfers between devices  413 us (53%)
  local copies, waits for them, and re-layouts  125 us (16%)
  starting transfers between devices  100 us (13%)
  matrix products  99.1 us (13%)
  between operations  14.4 us (2%)
  other arithmetic  10.3 us (1%)
    psum x1, waiting for transfers between devices, local(): grad_proj = lax.psum(proj_term.astype(jnp.bfloat16), 'dp')  172 us
    all_to_all x1, waiting for transfers between devices, local(): lax.all_to_all(back_keys.reshape(peer_count * capacity, piece_rows, piece...  102 us
    all_to_all x1, waiting for transfers between devices, local(): lax.all_to_all(send_keys, ('dp', 'fsdp'), split_axis=0, concat_axis=0, ti...  67 us
    all_to_all x1, waiting for transfers between devices, local(): lax.all_to_all(send_values, ('dp', 'fsdp'), split_axis=0, concat_axis=0,...  65.7 us
    all_to_all x1, starting transfers between devices, local(): lax.all_to_all(back_keys.reshape(peer_count * capacity, piece_rows, piece...  52.9 us
    unnamed x25, local copies, waits for them, and re-layouts  41 us
    dot_general x1, matrix products, local(): jnp.einsum('chqk,cqhd->ckhd', dscores, query_blocks, preferred_element_ty...  25.7 us
    dot_general x1, matrix products, local(): jnp.einsum('chqk,ckhd->cqhd', dscores, slot_keys, preferred_element_type=...  23.4 us
  transfers between devices with their start and end apart: 7, of which 5 were waited for; matrix products, arithmetic and copies ran while one was open for 22% of the time, Pallas kernels for 0%

commit v1 on v0

v1 whole, which is shorter than its diff:
```python
import functools
import math

import jax
import jax.numpy as jnp
from jax import lax
from jax.experimental import pallas as pl
from jax.experimental.pallas import tpu as pltpu
from jax.sharding import PartitionSpec as P

HEAD_DIM = 128
SPAN = 64
SLOTS = 2
LANES = 128
LOW = -1e30
BF16 = jnp.bfloat16
F32 = jnp.float32


def dot(a, b, dims):
    return lax.dot_general(a, b, ((dims[0], dims[1]), ((), ())), preferred_element_type=F32)


def neighbour_head(ref, n, cols):
    return jnp.concatenate([ref[p, n, :, cols] for p in range(ref.shape[0])], axis=0)


def stats_kernel(heads, scale, nbr_ref, live_ref, q_ref, up_ref, k_ref, v_ref, out_ref):
    count = q_ref.shape[0]
    base = pl.program_id(0) * count
    lane = lax.broadcasted_iota(jnp.int32, (SPAN, LANES), 1)

    def slot(r, carry):
        n = nbr_ref[base + r]
        live = live_ref[base + r] != 0

        @pl.when(live)
        def _():
            first = jnp.zeros((SPAN, LANES), F32)
            second = jnp.zeros((SPAN, LANES), F32)
            for h in range(heads):
                cols = slice(h * HEAD_DIM, (h + 1) * HEAD_DIM)
                scores = dot(q_ref[r, :, cols], neighbour_head(k_ref, n, cols), ((1,), (1,))) * scale
                dprobs = dot(up_ref[r, :, cols], neighbour_head(v_ref, n, cols), ((1,), (1,)))
                peak = jnp.max(scores, axis=1, keepdims=True)
                expo = jnp.exp(scores - peak)
                total = jnp.sum(expo, axis=1, keepdims=True)
                weighted = jnp.sum(expo * dprobs, axis=1, keepdims=True)
                first = jnp.where(lane == h, peak, first)
                first = jnp.where(lane == heads + h, weighted, first)
                second = jnp.where(lane == h, total, second)
            both = jnp.concatenate([first, second], axis=0)
            out_ref[r] = both.T[:8, :]

        @pl.when(jnp.logical_not(live))
        def _():
            out_ref[r] = jnp.zeros((8, LANES), F32)

        return carry

    lax.fori_loop(0, count, slot, 0)


def grads_kernel(heads, scale, nbr_ref, live_ref, where_ref, on_ref, stats_ref, q_ref, up_ref, k_ref, v_ref,
                 o_ref, gq_ref, gk_ref, gv_ref, acc_k, acc_v):
    count = q_ref.shape[0]
    step = pl.program_id(0)
    base = step * count
    pieces, _, piece_rows, _ = k_ref.shape

    @pl.when(step == 0)
    def _():
        acc_k[...] = jnp.zeros_like(acc_k)
        acc_v[...] = jnp.zeros_like(acc_v)

    def slot(r, carry):
        n = nbr_ref[base + r]
        live = live_ref[base + r] != 0

        @pl.when(live)
        def _():
            peaks, totals, weights = [], [], []
            for s in range(SLOTS):
                at = (base + r) * SLOTS + s
                tile = stats_ref[where_ref[at]]
                on = on_ref[at] != 0
                peaks.append(jnp.where(on, tile[:heads, :SPAN], LOW))
                totals.append(jnp.where(on, tile[:heads, SPAN:], 0.0))
                weights.append(jnp.where(on, tile[heads : 2 * heads, :SPAN], 0.0))
            peak = functools.reduce(jnp.maximum, peaks)
            factors = [jnp.exp(p - peak) for p in peaks]
            total = sum(f * t for f, t in zip(factors, totals))
            weighted = sum(f * w for f, w in zip(factors, weights))
            joined = jnp.concatenate([peak + jnp.log(total), weighted / total], axis=1)
            columns = jnp.concatenate([joined, jnp.zeros((LANES - heads, LANES), F32)], axis=0).T
            for h in range(heads):
                cols = slice(h * HEAD_DIM, (h + 1) * HEAD_DIM)
                q, up = q_ref[r, :, cols], up_ref[r, :, cols]
                keys, values = neighbour_head(k_ref, n, cols), neighbour_head(v_ref, n, cols)
                scores = dot(q, keys, ((1,), (1,))) * scale
                dprobs = dot(up, values, ((1,), (1,)))
                probs = jnp.exp(scores - columns[:SPAN, h : h + 1])
                probs_b = probs.astype(BF16)
                dscores = (probs * (dprobs - columns[SPAN:, h : h + 1]) * scale).astype(BF16)
                o_ref[r, :, cols] = dot(probs_b, values, ((1,), (0,))).astype(BF16)
                gq_ref[r, :, cols] = dot(dscores, keys, ((1,), (0,))).astype(BF16)
                acc_k[n, :, cols] += dot(dscores, q, ((0,), (0,)))
                acc_v[n, :, cols] += dot(probs_b, up, ((0,), (0,)))

        @pl.when(jnp.logical_not(live))
        def _():
            o_ref[r] = jnp.zeros(o_ref.shape[1:], BF16)
            gq_ref[r] = jnp.zeros(gq_ref.shape[1:], BF16)

        return carry

    lax.fori_loop(0, count, slot, 0)

    @pl.when(step == pl.num_programs(0) - 1)
    def _():
        def neighbour(n, carry):
            for p in range(pieces):
                rows = slice(p * piece_rows, (p + 1) * piece_rows)
                gk_ref[p, n] = acc_k[n, rows, :].astype(BF16)
                gv_ref[p, n] = acc_v[n, rows, :].astype(BF16)
            return carry

        lax.fori_loop(0, acc_k.shape[0], neighbour, 0)


def line_gather(x, axis):
    n = lax.axis_size(axis)
    rise = [(i, i + 1) for i in range(n - 1)]
    fall = [(i + 1, i) for i in range(n - 1)]
    ups, downs = [x], [x]
    for _ in range(n - 1):
        ups.append(lax.ppermute(ups[-1], axis, rise))
        downs.append(lax.ppermute(downs[-1], axis, fall))
    return [x] + [ups[r] + downs[n - r] for r in range(1, n)]


def swap(x, axis, bits):
    return lax.ppermute(x, axis, [(i, i ^ bits) for i in range(lax.axis_size(axis))])


def local(queries, nbr_keys, nbr_values, out_proj, nbr_source, nbr_index, nbr_count, cotangent):
    n_dp, n_f, n_e = lax.axis_size("dp"), lax.axis_size("fsdp"), lax.axis_size("enc")
    token_rows, width = queries.shape
    hw = width // n_f
    heads = hw // HEAD_DIM
    spans_here = token_rows // SPAN
    spans = spans_here * n_f
    slots = spans * SLOTS
    cap = (spans_here * SLOTS + n_dp - 1) // n_dp * n_f
    group, piece_rows, _ = nbr_keys.shape
    nbr_len = piece_rows * n_f
    bin_rows = token_rows * n_f
    homes = n_dp * cap
    scale = 1.0 / math.sqrt(HEAD_DIM)
    mine = lax.axis_index("dp")
    place = lax.axis_index("fsdp")
    enc = lax.axis_index("enc")

    src = nbr_source.reshape(n_dp, slots)
    idx = nbr_index.reshape(n_dp, slots)
    live = (jnp.arange(SLOTS, dtype=jnp.int32)[None, :] < nbr_count[:, None]).reshape(n_dp, slots)
    iota = jnp.arange(slots, dtype=jnp.int32)
    same = src[:, :, None] == src[:, None, :]
    rank = jnp.sum(jnp.logical_and(same, iota[None, None, :] < iota[None, :, None]), axis=2, dtype=jnp.int32)
    spot = src * cap + rank
    hit = spot[:, None, :] == jnp.arange(homes, dtype=jnp.int32)[None, :, None]
    inverse = jnp.sum(jnp.where(hit, iota[None, None, :], 0), axis=2).reshape(n_dp, n_dp, cap)
    present = jnp.any(hit, axis=2).reshape(n_dp, n_dp, cap)

    here = lax.dynamic_index_in_dim(inverse, mine, 1, keepdims=False)
    here_on = lax.dynamic_index_in_dim(present, mine, 1, keepdims=False)
    bins = jnp.arange(n_dp, dtype=jnp.int32)[:, None]
    home_nbr = idx[bins, here].reshape(homes)
    home_live = jnp.logical_and(here_on, live[bins, here]).astype(jnp.int32).reshape(homes)
    pair = (here // SLOTS * SLOTS)[:, :, None] + jnp.arange(SLOTS, dtype=jnp.int32)
    pair_spot = spot[bins[:, :, None], pair]
    pair_at = (pair_spot // cap * n_dp + bins[:, :, None]) * cap + pair_spot % cap
    pair_at = pair_at.astype(jnp.int32).reshape(homes * SLOTS)
    pair_on = live[bins[:, :, None], pair].astype(jnp.int32).reshape(homes * SLOTS)
    send_span = lax.dynamic_index_in_dim(inverse, mine, 0, keepdims=False).reshape(homes) // SLOTS
    my_spot = lax.dynamic_index_in_dim(spot, mine, 0, keepdims=False)
    my_live = lax.dynamic_index_in_dim(live, mine, 0, keepdims=False)

    def dispatch(x):
        chosen = jnp.take(x.reshape(spans, SPAN, hw), send_span, axis=0, mode="clip")
        return lax.all_to_all(chosen, "dp", split_axis=0, concat_axis=0, tiled=True)

    def collect(x):
        back = lax.all_to_all(x, "dp", split_axis=0, concat_axis=0, tiled=True)
        found = jnp.take(back, my_spot, axis=0, mode="clip")
        found = jnp.where(my_live[:, None, None], found.astype(F32), 0.0)
        return jnp.sum(found.reshape(spans, SLOTS, SPAN, hw), axis=1).astype(BF16).reshape(bin_rows, hw)

    def to_heads(x):
        split = x.reshape(group, piece_rows, n_f, hw).transpose(2, 0, 1, 3)
        return lax.all_to_all(split, "fsdp", split_axis=0, concat_axis=0, tiled=True)

    def to_rows(x):
        back = lax.all_to_all(x, "fsdp", split_axis=0, concat_axis=0, tiled=True)
        return back.transpose(1, 2, 0, 3).reshape(group, piece_rows, width)

    q_heads = lax.all_to_all(queries, "fsdp", split_axis=1, concat_axis=0, tiled=True)
    home_q = dispatch(q_heads)

    partial = dot(cotangent, out_proj, ((1,), (1,))).astype(BF16)
    parts = lax.all_to_all(
        partial.reshape(bin_rows, n_f, hw).transpose(1, 0, 2), "fsdp", split_axis=0, concat_axis=0, tiled=True
    )
    upstream = jnp.sum(parts.astype(F32), axis=0).astype(BF16)
    home_up = dispatch(upstream)

    keys = to_heads(nbr_keys)
    values = to_heads(nbr_values)

    slot_block = pl.BlockSpec((cap, SPAN, hw), lambda i, *_: (i, 0, 0))
    nbr_block = pl.BlockSpec((n_f, group, piece_rows, hw), lambda i, *_: (0, 0, 0, 0))
    stat_block = pl.BlockSpec((cap, 8, LANES), lambda i, *_: (i, 0, 0))
    params = pltpu.CompilerParams(vmem_limit_bytes=56 << 20)
    stats = pl.pallas_call(
        functools.partial(stats_kernel, heads, scale),
        grid_spec=pltpu.PrefetchScalarGridSpec(
            num_scalar_prefetch=2,
            grid=(n_dp,),
            in_specs=[slot_block, slot_block, nbr_block, nbr_block],
            out_specs=stat_block,
        ),
        out_shape=jax.ShapeDtypeStruct((homes, 8, LANES), F32),
        compiler_params=params,
    )(home_nbr, home_live, home_q, home_up, keys, values)
    all_stats = lax.all_gather(stats, "dp", axis=0, tiled=True)
    all_block = pl.BlockSpec((n_dp * homes, 8, LANES), lambda i, *_: (0, 0, 0))
    home_o, home_gq, grad_k, grad_v = pl.pallas_call(
        functools.partial(grads_kernel, heads, scale),
        grid_spec=pltpu.PrefetchScalarGridSpec(
            num_scalar_prefetch=4,
            grid=(n_dp,),
            in_specs=[all_block, slot_block, slot_block, nbr_block, nbr_block],
            out_specs=[slot_block, slot_block, nbr_block, nbr_block],
            scratch_shapes=[pltpu.VMEM((group, nbr_len, hw), F32), pltpu.VMEM((group, nbr_len, hw), F32)],
        ),
        out_shape=[
            jax.ShapeDtypeStruct((homes, SPAN, hw), BF16),
            jax.ShapeDtypeStruct((homes, SPAN, hw), BF16),
            jax.ShapeDtypeStruct((n_f, group, piece_rows, hw), BF16),
            jax.ShapeDtypeStruct((n_f, group, piece_rows, hw), BF16),
        ],
        compiler_params=params,
    )(home_nbr, home_live, pair_at, pair_on, all_stats, home_q, home_up, keys, values)

    attended_heads = collect(home_o)
    attended = lax.all_to_all(attended_heads, "fsdp", split_axis=0, concat_axis=1, tiled=True)
    grad_queries = lax.all_to_all(collect(home_gq), "fsdp", split_axis=0, concat_axis=1, tiled=True)
    grad_keys = to_rows(grad_k)
    grad_values = to_rows(grad_v)

    proj_cols = cotangent.shape[1]
    raw = (n_dp - 1) * bin_rows * (hw + proj_cols // n_e)
    summed = 2 * width * proj_cols * (n_dp - 1) // n_dp
    if raw <= summed and n_e == 2 and n_f % 2 == 0 and n_f & (n_f - 1) == 0:
        half = bin_rows // 2
        pieces = line_gather(lax.dynamic_slice_in_dim(cotangent, enc * half, half, 0), "dp")
        cots = [cotangent]
        for piece in pieces[1:]:
            other = swap(piece, "enc", 1)
            cots.append(jnp.where(enc == 0, piece, other))
            cots.append(jnp.where(enc == 0, other, piece))
        cot_all = jnp.concatenate(cots, axis=0)
        own = line_gather(attended_heads, "dp")
        grad_proj = jnp.zeros((width, proj_cols), BF16)
        for y in range(0, n_f, 2):
            even = own if y == 0 else [swap(piece, "fsdp", y) for piece in own]
            for bits, blocks in ((y, even), (y ^ 1, [swap(piece, "fsdp", 1) for piece in even])):
                term = dot(jnp.concatenate(blocks, axis=0), cot_all, ((0,), (0,))).astype(BF16)
                grad_proj = lax.dynamic_update_slice(grad_proj, term, ((place ^ bits) * hw, jnp.int32(0)))
    else:
        gathered = lax.all_gather(attended_heads, "fsdp", axis=1, tiled=True)
        grad_proj = lax.psum(dot(gathered, cotangent, ((0,), (0,))).astype(BF16), "dp")
    return (attended, grad_queries, grad_keys, grad_values, grad_proj)


def solution(mesh):
    placed = (
        P(("dp", "fsdp"), "enc"),
        P("dp", "fsdp", "enc"),
        P("dp", "fsdp", "enc"),
        P("enc", "fsdp"),
        P(),
        P(),
        P(),
        P("dp", "fsdp"),
    )
    return jax.shard_map(
        local,
        mesh=mesh,
        in_specs=placed,
        out_specs=(
            P(("dp", "fsdp"), "enc"),
            P(("dp", "fsdp"), "enc"),
            P("dp", "fsdp", "enc"),
            P("dp", "fsdp", "enc"),
            P("enc", "fsdp"),
        ),
        check_vma=False,
    )
```

time: 772 us -> 761 us (0.986); the launches traced: 762 us -> 765 us
  local copies, waits for them, and re-layouts: 125 us -> 51.5 us
  blocking collectives: 0 us -> 59.1 us
  matrix products: 99.1 us -> 42.1 us
  Pallas kernels: 0 us -> 53.4 us
  starting transfers between devices: 100 us -> 140 us
  waiting for transfers between devices: 413 us -> 378 us
  other arithmetic: 10.3 us -> 39.4 us
  between operations: 14.4 us -> 1.15 us
    ppermute x0 -> x27, waiting for transfers between devices: none -> 195 us  [the longest x6 127 us: line_gather(): downs.append(lax.ppermute(downs[-1], axis, fall))]
    psum x1 -> x0, waiting for transfers between devices: 172 us -> none  [local(): grad_proj = lax.psum(proj_term.astype(jnp.bfloat16), 'dp')]
    ppermute x0 -> x27, starting transfers between devices: none -> 81.2 us  [the longest x6 64.1 us: line_gather(): ups.append(lax.ppermute(ups[-1], axis, rise))]
    dot_general x12 -> x5, matrix products: 99.1 us -> 42.1 us  [dot(): lax.dot_general(a, b, ((dims[0], dims[1]), ((), ())), preferred_element_t...]
    pallas_call x0 -> x2, Pallas kernels: none -> 53.4 us  [the longest x1 37.2 us: local(): pl.pallas_call(functools.partial(grads_kernel, heads, scale), grid_spec=p...]
    all_to_all x4 -> x11, waiting for transfers between devices: 234 us -> 183 us  [the longest x2 84.3 us: dispatch(): return lax.all_to_all(chosen, 'dp', split_axis=0, concat_axis=0, tiled=True)]
    all_to_all x0 -> x1, blocking collectives: none -> 42.3 us  [to_rows(): back = lax.all_to_all(x, 'fsdp', split_axis=0, concat_axis=0, tiled=True)]
    all_to_all x4 -> x11, starting transfers between devices: 99.7 us -> 59 us  [the longest x2 20.8 us: collect(): back = lax.all_to_all(x, 'dp', split_axis=0, concat_axis=0, tiled=True)]
  transfers between devices with their start and end apart: 7 -> 38, of which waited for: 5 -> 16; matrix products, arithmetic and copies ran while one was open for 22% -> 15% of each run, Pallas kernels for 0% -> 0%
where the time goes in v1:
time: 761 us; the launch traced here: 765 us
  waiting for transfers between devices  378 us (50%)
  starting transfers between devices  140 us (18%)
  blocking collectives  59.1 us (8%)
  Pallas kernels  53.4 us (7%)
  local copies, waits for them, and re-layouts  51.5 us (7%)
  matrix products  42.1 us (6%)
  other arithmetic  39.4 us (5%)
    ppermute x6, waiting for transfers between devices, line_gather(): downs.append(lax.ppermute(downs[-1], axis, fall))  127 us
    all_to_all x2, waiting for transfers between devices, dispatch(): return lax.all_to_all(chosen, 'dp', split_axis=0, concat_axis=0, tiled=True)  84.3 us
    all_to_all x2, waiting for transfers between devices, to_heads(): lax.all_to_all(split, 'fsdp', split_axis=0, concat_axis=0, tiled=True)  66 us
    ppermute x6, starting transfers between devices, line_gather(): ups.append(lax.ppermute(ups[-1], axis, rise))  64.1 us
    ppermute x15, waiting for transfers between devices, swap(): lax.ppermute(x, axis, [(i, i ^ bits) for i in range(lax.axis_size(axis))])  44.9 us
    all_to_all x1, blocking collectives, to_rows(): back = lax.all_to_all(x, 'fsdp', split_axis=0, concat_axis=0, tiled=True)  42.3 us
    dot_general x5, matrix products, dot(): lax.dot_general(a, b, ((dims[0], dims[1]), ((), ())), preferred_element_t...  42.1 us
    pallas_call x1, Pallas kernels, local(): pl.pallas_call(functools.partial(grads_kernel, heads, scale), grid_spec=p...  37.2 us
  transfers between devices with their start and end apart: 38, of which 16 were waited for; matrix products, arithmetic and copies ran while one was open for 15% of the time, Pallas kernels for 0%

profile of v1, /device:TPU:0, one launch (start us, length us, event | category | flops | bytes accessed | tf_op | source)
XLA Modules:
  0.0 765.2 jit_solution(10825441127322101585)
XLA Ops:
  0.6 2.1 copy.70
  2.7 4.2 all-to-all-start
  7.0 10.1 %convolution_convert_fusion = bf16[768,2048]{1,0:T(8,128)(2,1)S(1)} fusion(bf16[768,2048]{1,0:T(8,128)(2,1)} %param.15, bf16[2048,2048]{1,0:T(8,128)(2,1)} %param.11), kind=kOutput, calls=%fused_computation.8 | convolution fusion | flops 6444023808 | bytes 14680064 | tf_op jit(solution)/shard_map/dot_general | solution.py:21
  17.0 2.0 copy.69
  19.9 3.7 all-to-all-start.2
  23.6 4.0 copy.68
  27.6 32.9 %all-to-all-done.2 = bf16[4,768,512]{2,1,0:T(8,128)(2,1)S(1)} async-done(((bf16[4,768,512]{2,1,0:T(8,128)(2,1)}), bf16[4,768,512]{2,1,0:T(8,128)(2,1)S(1)}, u32[]{:S(2)}, u32[]{:S(2)}) %all-to-all-start.2) | async-done | bytes 3145760 | tf_op jit(solution)/shard_map/all_to_all | solution.py:211
  62.2 3.7 all-to-all-start.4
  65.9 4.0 copy.67
  69.9 32.9 %all-to-all-done.4.k_ref = bf16[4,24,32,512]{3,2,1,0:T(8,128)(2,1)S(1)} async-done(((bf16[4,24,32,512]{3,2,1,0:T(8,128)(2,1)}), bf16[4,24,32,512]{3,2,1,0:T(8,128)(2,1)S(1)}, u32[]{:S(2)}, u32[]{:S(2)}) %all-to-all-start.4) | async-done | bytes 3145760 | tf_op jit(solution)/shard_map/all_to_all | solution.py:201
  104.4 4.7 all-to-all-start.5
  109.8 3.2 gather_fusion.4
  113.0 33.1 %all-to-all-done.5.v_ref = bf16[4,24,32,512]{3,2,1,0:T(8,128)(2,1)} async-done(((bf16[4,24,32,512]{3,2,1,0:T(8,128)(2,1)}), bf16[4,24,32,512]{3,2,1,0:T(8,128)(2,1)}, u32[]{:S(2)}, u32[]{:S(2)}) %all-to-all-start.5) | async-done | bytes 3145760 | tf_op jit(solution)/shard_map/all_to_all | solution.py:201
  146.1 5.6 all-to-all-start.1
  151.7 2.8 reduce_sum.50
  154.5 2.0 gather_fusion.5
  156.5 43.2 %all-to-all-done.1.q_ref = bf16[32,64,512]{2,1,0:T(8,128)(2,1)S(1)} async-done(((bf16[32,64,512]{2,1,0:T(8,128)(2,1)}), bf16[32,64,512]{2,1,0:T(8,128)(2,1)S(1)}, u32[]{:S(2)}, u32[]{:S(2)}) %all-to-all-start.1) | async-done | bytes 2097184 | tf_op jit(solution)/shard_map/all_to_all | solution.py:191
  199.7 4.4 all-to-all-start.3
  210.7 41.2 %all-to-all-done.3.up_ref = bf16[32,64,512]{2,1,0:T(8,128)(2,1)} async-done(((bf16[32,64,512]{2,1,0:T(8,128)(2,1)}), bf16[32,64,512]{2,1,0:T(8,128)(2,1)}, u32[]{:S(2)}, u32[]{:S(2)}) %all-to-all-start.3) | async-done | bytes 2097184 | tf_op jit(solution)/shard_map/all_to_all | solution.py:191
  251.9 16.2 %shard_map.119 = f32[32,8,128]{2,1,0:T(8,128)} custom-call(s32[32]{0:T(128)} %gather_fusion, s32[32]{0:T(128)} %and_convert_fusion.live_ref, bf16[32,64,512]{2,1,0:T(8,128)(2,1)} %copy-done.1, bf16[32,64,512]{2,1,0:T(8,128)(2,1)} %all-to-all-done.3.up_ref, bf16[4,24,32,512]{3,2,1,0:T(8,128)(2,1)} %copy-done, bf16[4,24,32,512]{3,2,1,0:T(8,128)(2,1)} %all-to-all-done.5.v_ref), custom_call_target="tpu_custom_call" | custom-call | tf_op jit(solution)/shard_map/pallas_call | solution.py:224
  268.1 16.8 %all_gather.3.stats_ref = f32[128,8,128]{2,1,0:T(8,128)} all-gather(f32[32,8,128]{2,1,0:T(8,128)} %shard_map.119), channel_id=1, replica_groups=mesh['dp'=4,'fsdp'=4,'enc'=2] {'dp'}, dimensions={0}, use_global_device_ids=true | all-gather | bytes 655360 | tf_op jit(solution)/shard_map/all_gather | solution.py:235
  284.9 37.2 %shard_map.120 = (bf16[32,64,512]{2,1,0:T(8,128)(2,1)}, bf16[32,64,512]{2,1,0:T(8,128)(2,1)}, bf16[4,24,32,512]{3,2,1,0:T(8,128)(2,1)}, bf16[4,24,32,512]{3,2,1,0:T(8,128)(2,1)}) custom-call(s32[32]{0:T(128)} %gather_fusion, s32[32]{0:T(128)} %and_convert_fusion.live_ref, s32[64]{0:T(128)} %fusion.68.where_ref, s32[64]{0:T(128)} %convert_element_type.85.on_ref, ...), custom_call_target="tpu_custom_call" | custom-call | tf_op jit(solution)/shard_map/pallas_call | solution.py:237
  322.1 42.3 %all_to_all.93 = bf16[4,24,32,512]{3,2,1,0:T(8,128)(2,1)} all-to-all(bf16[4,24,32,512]{3,2,1,0:T(8,128)(2,1)} %get-tuple-element.11), channel_id=1, replica_groups=mesh['dp'=4,'fsdp'=4,'enc'=2] {'fsdp'}, dimensions={0} | all-to-all | bytes 6291456 | tf_op jit(solution)/shard_map/all_to_all | solution.py:204
  364.3 4.7 all-to-all-start.6
  371.6 5.7 collective-permute-start.6
  377.3 61.3 %collective-permute-done.7 = bf16[384,2048]{1,0:T(8,128)(2,1)S(1)} collective-permute-done((bf16[384,2048]{1,0:T(8,128)(2,1)}, bf16[384,2048]{1,0:T(8,128)(2,1)S(1)}, u32[]{:S(2)}, u32[]{:S(2)}) %collective-permute-start.7) | collective-permute-done | bytes 1572896 | tf_op jit(solution)/shard_map/ppermute | solution.py:138
  440.0 16.1 %all-to-all-start.8 = ((bf16[32,64,512]{2,1,0:T(8,128)(2,1)}), bf16[32,64,512]{2,1,0:T(8,128)(2,1)}, u32[]{:S(2)}, u32[]{:S(2)}) async-start(bf16[32,64,512]{2,1,0:T(8,128)(2,1)} %get-tuple-element.10), calls=%async_computation.8 | async-start | bytes 4194304 | tf_op jit(solution)/shard_map/all_to_all | solution.py:194
  456.1 5.1 collective-permute-start.11
  461.2 38.1 %collective-permute-done.8 = bf16[384,2048]{1,0:T(8,128)(2,1)S(1)} collective-permute-done((bf16[384,2048]{1,0:T(8,128)(2,1)S(1)}, bf16[384,2048]{1,0:T(8,128)(2,1)S(1)}, u32[]{:S(2)}, u32[]{:S(2)}) %collective-permute-start.8) | collective-permute-done | bytes 1572896 | tf_op jit(solution)/shard_map/ppermute | solution.py:138
  500.6 22.2 %collective-permute-done.11 = bf16[384,2048]{1,0:T(8,128)(2,1)} collective-permute-done((bf16[384,2048]{1,0:T(8,128)(2,1)}, bf16[384,2048]{1,0:T(8,128)(2,1)}, u32[]{:S(2)}, u32[]{:S(2)}) %collective-permute-start.11) | collective-permute-done | bytes 1572896 | tf_op jit(solution)/shard_map/ppermute | solution.py:137
  522.7 16.6 %collective-permute-start.13 = (bf16[384,2048]{1,0:T(8,128)(2,1)}, bf16[384,2048]{1,0:T(8,128)(2,1)}, u32[]{:S(2)}, u32[]{:S(2)}) collective-permute-start(bf16[384,2048]{1,0:T(8,128)(2,1)} %collective-permute-done.11), channel_id=1, source_target_pairs={{0,8},{8,16},{16,24},{1,9},{9,17},{17,25},{2,10},{10,18},{18,26},{... | collective-permute-start | bytes 4718600 | tf_op jit(solution)/shard_map/ppermute | solution.py:137
  539.3 15.0 %collective-permute-done.9 = bf16[384,2048]{1,0:T(8,128)(2,1)S(1)} collective-permute-done((bf16[384,2048]{1,0:T(8,128)(2,1)S(1)}, bf16[384,2048]{1,0:T(8,128)(2,1)S(1)}, u32[]{:S(2)}, u32[]{:S(2)}) %collective-permute-start.9) | collective-permute-done | bytes 1572896 | tf_op jit(solution)/shard_map/ppermute | solution.py:138
  554.3 2.0 add.151
  557.9 4.8 all-to-all-start.11
  563.0 3.9 constant_dynamic-update-slice_fusion
  567.0 3.3 add.152
  570.9 2.0 add.153
  574.4 3.4 gather_fusion.6
  577.9 3.4 gather_fusion.7
  581.3 4.3 fusion.32
  586.9 16.5 %collective-permute-start = (bf16[768,512]{1,0:T(8,128)(2,1)}, bf16[768,512]{1,0:T(8,128)(2,1)}, u32[]{:S(2)}, u32[]{:S(2)}) collective-permute-start(bf16[768,512]{1,0:T(8,128)(2,1)} %bitcast.19), channel_id=1, source_target_pairs={{0,8},{8,16},{16,24},{1,9},{9,17},{17,25},{2,10},{10,18},{18,26},{... | collective-permute-start | bytes 2359304 | tf_op jit(solution)/shard_map/ppermute | solution.py:137
  605.1 3.2 select_dynamic-update-slice_fusion.4
  608.4 9.9 %collective-permute-done.1 = bf16[768,512]{1,0:T(8,128)(2,1)} collective-permute-done((bf16[768,512]{1,0:T(8,128)(2,1)}, bf16[768,512]{1,0:T(8,128)(2,1)}, u32[]{:S(2)}, u32[]{:S(2)}) %collective-permute-start.1) | collective-permute-done | bytes 786464 | tf_op jit(solution)/shard_map/ppermute | solution.py:138
  619.6 4.6 collective-permute-start.4
  624.2 3.5 all-to-all-start.7
  627.7 3.3 select_dynamic-update-slice_fusion.3
  631.0 3.3 select_dynamic-update-slice_fusion.2
  636.4 2.6 collective-permute-done.2
  640.2 2.5 add.148
  644.0 3.5 all-to-all-start.9
  647.5 11.1 %collective-permute-done.14 = bf16[384,2048]{1,0:T(8,128)(2,1)} collective-permute-done((bf16[384,2048]{1,0:T(8,128)(2,1)S(1)}, bf16[384,2048]{1,0:T(8,128)(2,1)}, u32[]{:S(2)}, u32[]{:S(2)}) %collective-permute-start.14) | collective-permute-done | bytes 1572896 | tf_op jit(solution)/shard_map/ppermute | solution.py:143
  658.6 15.6 %collective-permute-start.5 = (bf16[768,512]{1,0:T(8,128)(2,1)}, bf16[768,512]{1,0:T(8,128)(2,1)}, u32[]{:S(2)}, u32[]{:S(2)}) collective-permute-start(bf16[768,512]{1,0:T(8,128)(2,1)} %copy-done.10), channel_id=1, source_target_pairs={{0,8},{8,16},{16,24},{1,9},{9,17},{17,25},{2,10},{10,18},{18,26},{... | collective-permute-start | bytes 2359304 | tf_op jit(solution)/shard_map/ppermute | solution.py:137
  676.0 3.4 select_dynamic-update-slice_fusion
  679.4 2.1 copy.61
  681.5 4.0 copy.62
  690.3 1.9 add.149
  695.5 8.3 %fusion.55 = bf16[2048,2048]{1,0:T(8,128)(2,1)S(1)} fusion(bf16[2048,2048]{1,0:T(8,128)(2,1)S(1)} %broadcast_in_dim.81, s32[]{:T(128)S(6)} %select_n.147, bf16[3072,2048]{1,0:T(8,128)(2,1)S(1)} %copy-done.9, bf16[768,512]{1,0:T(8,128)(2,1)S(1)} %add.149, bf16[768,512]{1,0:T(8,128)(2,1)} %add.148, bf16[768,512]{1,0:T(8,128)(2,1)S(1)} %add.147, ...), kind=kOutput, calls=%fused_computation.55 | convolution fusion | flops 6456082432 | bytes 17825796 | tf_op jit(solution)/shard_map/dot_general | solution.py:21
  703.7 4.6 collective-permute-done.21
  708.8 16.3 %collective-permute-done.20 = bf16[768,512]{1,0:T(8,128)(2,1)} collective-permute-done((bf16[768,512]{1,0:T(8,128)(2,1)S(1)}, bf16[768,512]{1,0:T(8,128)(2,1)}, u32[]{:S(2)}, u32[]{:S(2)}) %collective-permute-start.20) | collective-permute-done | bytes 786464 | tf_op jit(solution)/shard_map/ppermute | solution.py:143
  725.2 12.8 %collective-permute-done.22 = bf16[768,512]{1,0:T(8,128)(2,1)} collective-permute-done((bf16[768,512]{1,0:T(8,128)(2,1)S(1)}, bf16[768,512]{1,0:T(8,128)(2,1)}, u32[]{:S(2)}, u32[]{:S(2)}) %collective-permute-start.22) | collective-permute-done | bytes 786464 | tf_op jit(solution)/shard_map/ppermute | solution.py:143
  738.0 8.3 %fusion.49 = bf16[2048,2048]{1,0:T(8,128)(2,1)S(1)} fusion(bf16[2048,2048]{1,0:T(8,128)(2,1)S(1)} %fusion.55, s32[]{:T(128)S(6)} %select_n.148, bf16[3072,2048]{1,0:T(8,128)(2,1)S(1)} %copy-done.9, bf16[768,512]{1,0:T(8,128)(2,1)} %collective-permute-done.18, bf16[768,512]{1,0:T(8,128)(2,1)} %collective-permute-done.17, ...), kind=kOutput, calls=%fused_computation.53 | convolution fusion | flops 6456082432 | bytes 17825796 | tf_op jit(solution)/shard_map/dot_general | solution.py:21
  746.3 8.3 %fusion.43 = bf16[2048,2048]{1,0:T(8,128)(2,1)S(1)} fusion(bf16[2048,2048]{1,0:T(8,128)(2,1)S(1)} %fusion.49, s32[]{:T(128)S(6)} %select_n.149, bf16[3072,2048]{1,0:T(8,128)(2,1)S(1)} %copy-done.9, bf16[768,512]{1,0:T(8,128)(2,1)} %collective-permute-done.22, bf16[768,512]{1,0:T(8,128)(2,1)} %collective-permute-done.21, ...), kind=kOutput, calls=%fused_computation.51 | convolution fusion | flops 6456082432 | bytes 17825796 | tf_op jit(solution)/shard_map/dot_general | solution.py:21
  754.7 7.1 fusion.37
  761.8 3.4 copy-done.5
  (120 shorter events, 39.6 us)
Async XLA Ops:
  2.7 16.3 %all-to-all-start = ((bf16[192,4,512]{2,0,1:T(8,128)(2,1)}), bf16[192,4,512]{2,0,1:T(8,128)(2,1)S(1)}, u32[]{:S(2)}, u32[]{:S(2)}) async-start(bf16[192,4,512]{2,0,1:T(8,128)(2,1)} %bitcast.66), calls=%async_computation | async-start | bytes 1572864 | tf_op jit(solution)/shard_map/all_to_all | solution.py:207
  19.0 0.9 copy-start.4
  19.9 40.6 %all-to-all-start.2 = ((bf16[4,768,512]{2,1,0:T(8,128)(2,1)}), bf16[4,768,512]{2,1,0:T(8,128)(2,1)S(1)}, u32[]{:S(2)}, u32[]{:S(2)}) async-start(bf16[4,768,512]{2,1,0:T(8,128)(2,1)} %bitcast.69), calls=%async_computation.2 | async-start | bytes 6291456 | tf_op jit(solution)/shard_map/all_to_all | solution.py:211
  60.5 1.7 copy-start.3
  62.2 40.6 %all-to-all-start.4 = ((bf16[4,24,32,512]{3,2,1,0:T(8,128)(2,1)}), bf16[4,24,32,512]{3,2,1,0:T(8,128)(2,1)S(1)}, u32[]{:S(2)}, u32[]{:S(2)}) async-start(bf16[4,24,32,512]{3,2,1,0:T(8,128)(2,1)} %bitcast.70), calls=%async_computation.4 | async-start | bytes 6291456 | tf_op jit(solution)/shard_map/all_to_all | solution.py:201
  102.8 1.7 copy-start
  102.8 6.3 copy-start.11
  104.4 41.7 %all-to-all-start.5 = ((bf16[4,24,32,512]{3,2,1,0:T(8,128)(2,1)}), bf16[4,24,32,512]{3,2,1,0:T(8,128)(2,1)}, u32[]{:S(2)}, u32[]{:S(2)}) async-start(bf16[4,24,32,512]{3,2,1,0:T(8,128)(2,1)} %bitcast.68), calls=%async_computation.5 | async-start | bytes 6291456 | tf_op jit(solution)/shard_map/all_to_all | solution.py:201
  146.1 53.6 %all-to-all-start.1 = ((bf16[32,64,512]{2,1,0:T(8,128)(2,1)}), bf16[32,64,512]{2,1,0:T(8,128)(2,1)S(1)}, u32[]{:S(2)}, u32[]{:S(2)}) async-start(bf16[32,64,512]{2,1,0:T(8,128)(2,1)} %gather_fusion.4), calls=%async_computation.1 | async-start | bytes 4194304 | tf_op jit(solution)/shard_map/all_to_all | solution.py:191
  156.5 47.7 %copy-start.13 = (s32[48]{0:T(128)S(1)}, s32[48]{0:T(128)}, u32[]{:S(2)}) copy-start(s32[48]{0:T(128)} %param.14) | copy-start | bytes 580
  199.7 5.9 copy-start.1
  199.7 52.2 %all-to-all-start.3 = ((bf16[32,64,512]{2,1,0:T(8,128)(2,1)}), bf16[32,64,512]{2,1,0:T(8,128)(2,1)}, u32[]{:S(2)}, u32[]{:S(2)}) async-start(bf16[32,64,512]{2,1,0:T(8,128)(2,1)} %gather_fusion.5), calls=%async_computation.3 | async-start | bytes 4194304 | tf_op jit(solution)/shard_map/all_to_all | solution.py:191
  205.6 2.0 copy-start.12
  364.3 4.7 copy-start.6
  364.3 75.7 %all-to-all-start.6 = ((bf16[32,64,512]{2,1,0:T(8,128)(2,1)}), bf16[32,64,512]{2,1,0:T(8,128)(2,1)}, u32[]{:S(2)}, u32[]{:S(2)}) async-start(bf16[32,64,512]{2,1,0:T(8,128)(2,1)} %get-tuple-element.9), calls=%async_computation.6 | async-start | bytes 4194304 | tf_op jit(solution)/shard_map/all_to_all | solution.py:194
  370.3 68.4 %collective-permute-start.7 = (bf16[384,2048]{1,0:T(8,128)(2,1)}, bf16[384,2048]{1,0:T(8,128)(2,1)S(1)}, u32[]{:S(2)}, u32[]{:S(2)}) collective-permute-start(bf16[384,2048]{1,0:T(8,128)(2,1)} %constant_dynamic-slice_fusion), channel_id=1, source_target_pairs={{8,0},{16,8},{24,16},{9,1},{17,9},{25,17},{10,2},{18,10},{26,18},{... | collective-permute-start | bytes 4718600 | tf_op jit(solution)/shard_map/ppermute | solution.py:138
  371.6 84.5 %collective-permute-start.6 = (bf16[384,2048]{1,0:T(8,128)(2,1)}, bf16[384,2048]{1,0:T(8,128)(2,1)}, u32[]{:S(2)}, u32[]{:S(2)}) collective-permute-start(bf16[384,2048]{1,0:T(8,128)(2,1)} %constant_dynamic-slice_fusion), channel_id=1, source_target_pairs={{0,8},{8,16},{16,24},{1,9},{9,17},{17,25},{2,10},{10,18},{18,26},{... | collective-permute-start | bytes 4718600 | tf_op jit(solution)/shard_map/ppermute | solution.py:137
  438.7 100.6 %copy-start.7 = (bf16[384,2048]{1,0:T(8,128)(2,1)}, bf16[384,2048]{1,0:T(8,128)(2,1)S(1)}, u32[]{:S(2)}) copy-start(bf16[384,2048]{1,0:T(8,128)(2,1)S(1)} %collective-permute-done.7) | copy-start | bytes 4718596
  438.7 60.6 %collective-permute-start.8 = (bf16[384,2048]{1,0:T(8,128)(2,1)S(1)}, bf16[384,2048]{1,0:T(8,128)(2,1)S(1)}, u32[]{:S(2)}, u32[]{:S(2)}) collective-permute-start(bf16[384,2048]{1,0:T(8,128)(2,1)S(1)} %collective-permute-done.7), channel_id=1, source_target_pairs={{8,0},{16,8},{24,16},{9,1},{17,9},{25,17},{10,2},{18,10},{26,18},{... | collective-permute-start | bytes 4718600 | tf_op jit(solution)/shard_map/ppermute | solution.py:138
  440.0 117.9 %all-to-all-start.8 = ((bf16[32,64,512]{2,1,0:T(8,128)(2,1)}), bf16[32,64,512]{2,1,0:T(8,128)(2,1)}, u32[]{:S(2)}, u32[]{:S(2)}) async-start(bf16[32,64,512]{2,1,0:T(8,128)(2,1)} %get-tuple-element.10), calls=%async_computation.8 | async-start | bytes 4194304 | tf_op jit(solution)/shard_map/all_to_all | solution.py:194
  456.1 66.6 %collective-permute-start.11 = (bf16[384,2048]{1,0:T(8,128)(2,1)}, bf16[384,2048]{1,0:T(8,128)(2,1)}, u32[]{:S(2)}, u32[]{:S(2)}) collective-permute-start(bf16[384,2048]{1,0:T(8,128)(2,1)} %collective-permute-done.6), channel_id=1, source_target_pairs={{0,8},{8,16},{16,24},{1,9},{9,17},{17,25},{2,10},{10,18},{18,26},{... | collective-permute-start | bytes 4718600 | tf_op jit(solution)/shard_map/ppermute | solution.py:137
  499.3 55.1 %collective-permute-start.9 = (bf16[384,2048]{1,0:T(8,128)(2,1)S(1)}, bf16[384,2048]{1,0:T(8,128)(2,1)S(1)}, u32[]{:S(2)}, u32[]{:S(2)}) collective-permute-start(bf16[384,2048]{1,0:T(8,128)(2,1)S(1)} %collective-permute-done.8), channel_id=1, source_target_pairs={{8,0},{16,8},{24,16},{9,1},{17,9},{25,17},{10,2},{18,10},{26,18},{... | collective-permute-start | bytes 4718600 | tf_op jit(solution)/shard_map/ppermute | solution.py:138
  522.7 48.1 %collective-permute-start.13 = (bf16[384,2048]{1,0:T(8,128)(2,1)}, bf16[384,2048]{1,0:T(8,128)(2,1)}, u32[]{:S(2)}, u32[]{:S(2)}) collective-permute-start(bf16[384,2048]{1,0:T(8,128)(2,1)} %collective-permute-done.11), channel_id=1, source_target_pairs={{0,8},{8,16},{16,24},{1,9},{9,17},{17,25},{2,10},{10,18},{18,26},{... | collective-permute-start | bytes 4718600 | tf_op jit(solution)/shard_map/ppermute | solution.py:137
  556.3 47.0 %collective-permute-start.10 = (bf16[384,2048]{1,0:T(8,128)(2,1)S(1)}, bf16[384,2048]{1,0:T(8,128)(2,1)}, u32[]{:S(2)}, u32[]{:S(2)}) collective-permute-start(bf16[384,2048]{1,0:T(8,128)(2,1)S(1)} %add.151), channel_id=1, source_target_pairs={{0,1},{1,0},{2,3},{3,2},{4,5},{5,4},{6,7},{7,6},{8,9},{9,8},{10,11... | collective-permute-start | bytes 4718600 | tf_op jit(solution)/shard_map/ppermute | solution.py:143
  557.9 66.3 %all-to-all-start.11 = ((bf16[4,24,32,512]{3,2,1,0:T(8,128)(2,1)}), bf16[4,24,32,512]{3,2,1,0:T(8,128)(2,1)}, u32[]{:S(2)}, u32[]{:S(2)}) async-start(bf16[4,24,32,512]{3,2,1,0:T(8,128)(2,1)} %get-tuple-element.12), calls=%async_computation.11 | async-start | bytes 6291456 | tf_op jit(solution)/shard_map/all_to_all | solution.py:204
  567.0 3.9 copy-start.8
  570.3 57.4 %collective-permute-start.12 = (bf16[384,2048]{1,0:T(8,128)(2,1)}, bf16[384,2048]{1,0:T(8,128)(2,1)}, u32[]{:S(2)}, u32[]{:S(2)}) collective-permute-start(bf16[384,2048]{1,0:T(8,128)(2,1)} %add.152), channel_id=1, source_target_pairs={{0,1},{1,0},{2,3},{3,2},{4,5},{5,4},{6,7},{7,6},{8,9},{9,8},{10,11... | collective-permute-start | bytes 4718600 | tf_op jit(solution)/shard_map/ppermute | solution.py:143
  572.9 85.7 %collective-permute-start.14 = (bf16[384,2048]{1,0:T(8,128)(2,1)S(1)}, bf16[384,2048]{1,0:T(8,128)(2,1)}, u32[]{:S(2)}, u32[]{:S(2)}) collective-permute-start(bf16[384,2048]{1,0:T(8,128)(2,1)S(1)} %add.153), channel_id=1, source_target_pairs={{0,1},{1,0},{2,3},{3,2},{4,5},{5,4},{6,7},{7,6},{8,9},{9,8},{10,11... | collective-permute-start | bytes 4718600 | tf_op jit(solution)/shard_map/ppermute | solution.py:143
  585.6 32.6 %collective-permute-start.1 = (bf16[768,512]{1,0:T(8,128)(2,1)}, bf16[768,512]{1,0:T(8,128)(2,1)}, u32[]{:S(2)}, u32[]{:S(2)}) collective-permute-start(bf16[768,512]{1,0:T(8,128)(2,1)} %bitcast.19), channel_id=1, source_target_pairs={{8,0},{16,8},{24,16},{9,1},{17,9},{25,17},{10,2},{18,10},{26,18},{... | collective-permute-start | bytes 2359304 | tf_op jit(solution)/shard_map/ppermute | solution.py:138
  586.9 32.6 %collective-permute-start = (bf16[768,512]{1,0:T(8,128)(2,1)}, bf16[768,512]{1,0:T(8,128)(2,1)}, u32[]{:S(2)}, u32[]{:S(2)}) collective-permute-start(bf16[768,512]{1,0:T(8,128)(2,1)} %bitcast.19), channel_id=1, source_target_pairs={{0,8},{8,16},{16,24},{1,9},{9,17},{17,25},{2,10},{10,18},{18,26},{... | collective-permute-start | bytes 2359304 | tf_op jit(solution)/shard_map/ppermute | solution.py:137
  618.3 20.8 %collective-permute-start.2 = (bf16[768,512]{1,0:T(8,128)(2,1)}, bf16[768,512]{1,0:T(8,128)(2,1)}, u32[]{:S(2)}, u32[]{:S(2)}) collective-permute-start(bf16[768,512]{1,0:T(8,128)(2,1)} %collective-permute-done.1), channel_id=1, source_target_pairs={{8,0},{16,8},{24,16},{9,1},{17,9},{25,17},{10,2},{18,10},{26,18},{... | collective-permute-start | bytes 2359304 | tf_op jit(solution)/shard_map/ppermute | solution.py:138
  619.6 20.7 %collective-permute-start.4 = (bf16[768,512]{1,0:T(8,128)(2,1)}, bf16[768,512]{1,0:T(8,128)(2,1)S(1)}, u32[]{:S(2)}, u32[]{:S(2)}) collective-permute-start(bf16[768,512]{1,0:T(8,128)(2,1)} %collective-permute-done), channel_id=1, source_target_pairs={{0,8},{8,16},{16,24},{1,9},{9,17},{17,25},{2,10},{10,18},{18,26},{... | collective-permute-start | bytes 2359304 | tf_op jit(solution)/shard_map/ppermute | solution.py:137
  624.2 19.8 %all-to-all-start.7 = ((bf16[4,192,512]{2,1,0:T(8,128)(2,1)}), bf16[4,192,512]{2,1,0:T(8,128)(2,1)S(1)}, u32[]{:S(2)}, u32[]{:S(2)}) async-start(bf16[4,192,512]{2,1,0:T(8,128)(2,1)} %bitcast.12), calls=%async_computation.7 | async-start | bytes 1572864 | tf_op jit(solution)/shard_map/all_to_all | solution.py:256
  634.3 58.0 %collective-permute-start.15 = (bf16[768,512]{1,0:T(8,128)(2,1)}, bf16[768,512]{1,0:T(8,128)(2,1)}, u32[]{:S(2)}, u32[]{:S(2)}) collective-permute-start(bf16[768,512]{1,0:T(8,128)(2,1)} %bitcast.19), channel_id=1, source_target_pairs={{0,2},{2,0},{4,6},{6,4},{1,3},{3,1},{5,7},{7,5},{8,10},{10,8},{12,... | collective-permute-start | bytes 2359304 | tf_op jit(solution)/shard_map/ppermute | solution.py:143
  634.7 58.7 %collective-permute-start.19 = (bf16[768,512]{1,0:T(8,128)(2,1)}, bf16[768,512]{1,0:T(8,128)(2,1)}, u32[]{:S(2)}, u32[]{:S(2)}) collective-permute-start(bf16[768,512]{1,0:T(8,128)(2,1)} %bitcast.19), channel_id=1, source_target_pairs={{0,4},{2,6},{4,0},{6,2},{1,5},{3,7},{5,1},{7,3},{8,12},{10,14},{12... | collective-permute-start | bytes 2359304 | tf_op jit(solution)/shard_map/ppermute | solution.py:143
  640.2 3.8 copy-start.10
  642.7 50.7 %collective-permute-start.17 = (bf16[768,512]{1,0:T(8,128)(2,1)}, bf16[768,512]{1,0:T(8,128)(2,1)}, u32[]{:S(2)}, u32[]{:S(2)}) collective-permute-start(bf16[768,512]{1,0:T(8,128)(2,1)} %add.148), channel_id=1, source_target_pairs={{0,2},{2,0},{4,6},{6,4},{1,3},{3,1},{5,7},{7,5},{8,10},{10,8},{12,... | collective-permute-start | bytes 2359304 | tf_op jit(solution)/shard_map/ppermute | solution.py:143
  642.7 44.8 %collective-permute-start.3 = (bf16[768,512]{1,0:T(8,128)(2,1)}, bf16[768,512]{1,0:T(8,128)(2,1)}, u32[]{:S(2)}, u32[]{:S(2)}) collective-permute-start(bf16[768,512]{1,0:T(8,128)(2,1)} %collective-permute-done.2), channel_id=1, source_target_pairs={{8,0},{16,8},{24,16},{9,1},{17,9},{25,17},{10,2},{18,10},{26,18},{... | collective-permute-start | bytes 2359304 | tf_op jit(solution)/shard_map/ppermute | solution.py:138
  644.0 42.5 %all-to-all-start.9 = ((bf16[4,192,512]{2,1,0:T(8,128)(2,1)}), bf16[4,192,512]{2,1,0:T(8,128)(2,1)S(1)}, u32[]{:S(2)}, u32[]{:S(2)}) async-start(bf16[4,192,512]{2,1,0:T(8,128)(2,1)} %bitcast.82), calls=%async_computation.9 | async-start | bytes 1572864 | tf_op jit(solution)/shard_map/all_to_all | solution.py:257
  658.6 31.6 %collective-permute-start.5 = (bf16[768,512]{1,0:T(8,128)(2,1)}, bf16[768,512]{1,0:T(8,128)(2,1)}, u32[]{:S(2)}, u32[]{:S(2)}) collective-permute-start(bf16[768,512]{1,0:T(8,128)(2,1)} %copy-done.10), channel_id=1, source_target_pairs={{0,8},{8,16},{16,24},{1,9},{9,17},{17,25},{2,10},{10,18},{18,26},{... | collective-permute-start | bytes 2359304 | tf_op jit(solution)/shard_map/ppermute | solution.py:137
  676.0 3.4 copy-start.2
  687.5 20.8 %collective-permute-start.21 = (bf16[768,512]{1,0:T(8,128)(2,1)}, bf16[768,512]{1,0:T(8,128)(2,1)}, u32[]{:S(2)}, u32[]{:S(2)}) collective-permute-start(bf16[768,512]{1,0:T(8,128)(2,1)} %add.148), channel_id=1, source_target_pairs={{0,4},{2,6},{4,0},{6,2},{1,5},{3,7},{5,1},{7,3},{8,12},{10,14},{12... | collective-permute-start | bytes 2359304 | tf_op jit(solution)/shard_map/ppermute | solution.py:143
  688.4 7.0 copy-start.9
  690.2 18.1 %collective-permute-start.16 = (bf16[768,512]{1,0:T(8,128)(2,1)S(1)}, bf16[768,512]{1,0:T(8,128)(2,1)}, u32[]{:S(2)}, u32[]{:S(2)}) collective-permute-start(bf16[768,512]{1,0:T(8,128)(2,1)S(1)} %add.147), channel_id=1, source_target_pairs={{0,2},{2,0},{4,6},{6,4},{1,3},{3,1},{5,7},{7,5},{8,10},{10,8},{12,... | collective-permute-start | bytes 2359304 | tf_op jit(solution)/shard_map/ppermute | solution.py:143
  692.2 33.0 %collective-permute-start.20 = (bf16[768,512]{1,0:T(8,128)(2,1)S(1)}, bf16[768,512]{1,0:T(8,128)(2,1)}, u32[]{:S(2)}, u32[]{:S(2)}) collective-permute-start(bf16[768,512]{1,0:T(8,128)(2,1)S(1)} %add.147), channel_id=1, source_target_pairs={{0,4},{2,6},{4,0},{6,2},{1,5},{3,7},{5,1},{7,3},{8,12},{10,14},{12... | collective-permute-start | bytes 2359304 | tf_op jit(solution)/shard_map/ppermute | solution.py:143
  693.4 44.6 %collective-permute-start.18 = (bf16[768,512]{1,0:T(8,128)(2,1)S(1)}, bf16[768,512]{1,0:T(8,128)(2,1)}, u32[]{:S(2)}, u32[]{:S(2)}) collective-permute-start(bf16[768,512]{1,0:T(8,128)(2,1)S(1)} %add.149), channel_id=1, source_target_pairs={{0,2},{2,0},{4,6},{6,4},{1,3},{3,1},{5,7},{7,5},{8,10},{10,8},{12,... | collective-permute-start | bytes 2359304 | tf_op jit(solution)/shard_map/ppermute | solution.py:143
  693.4 44.6 %collective-permute-start.22 = (bf16[768,512]{1,0:T(8,128)(2,1)S(1)}, bf16[768,512]{1,0:T(8,128)(2,1)}, u32[]{:S(2)}, u32[]{:S(2)}) collective-permute-start(bf16[768,512]{1,0:T(8,128)(2,1)S(1)} %add.149), channel_id=1, source_target_pairs={{0,4},{2,6},{4,0},{6,2},{1,5},{3,7},{5,1},{7,3},{8,12},{10,14},{12... | collective-permute-start | bytes 2359304 | tf_op jit(solution)/shard_map/ppermute | solution.py:143
  708.3 46.3 %collective-permute-start.23 = (bf16[768,512]{1,0:T(8,128)(2,1)}, bf16[768,512]{1,0:T(8,128)(2,1)S(1)}, u32[]{:S(2)}, u32[]{:S(2)}) collective-permute-start(bf16[768,512]{1,0:T(8,128)(2,1)} %collective-permute-done.19), channel_id=1, source_target_pairs={{0,2},{2,0},{4,6},{6,4},{1,3},{3,1},{5,7},{7,5},{8,10},{10,8},{12,... | collective-permute-start | bytes 2359304 | tf_op jit(solution)/shard_map/ppermute | solution.py:143
  708.3 46.3 %collective-permute-start.25 = (bf16[768,512]{1,0:T(8,128)(2,1)}, bf16[768,512]{1,0:T(8,128)(2,1)S(1)}, u32[]{:S(2)}, u32[]{:S(2)}) collective-permute-start(bf16[768,512]{1,0:T(8,128)(2,1)} %collective-permute-done.21), channel_id=1, source_target_pairs={{0,2},{2,0},{4,6},{6,4},{1,3},{3,1},{5,7},{7,5},{8,10},{10,8},{12,... | collective-permute-start | bytes 2359304 | tf_op jit(solution)/shard_map/ppermute | solution.py:143
  725.2 29.5 %collective-permute-start.24 = (bf16[768,512]{1,0:T(8,128)(2,1)}, bf16[768,512]{1,0:T(8,128)(2,1)S(1)}, u32[]{:S(2)}, u32[]{:S(2)}) collective-permute-start(bf16[768,512]{1,0:T(8,128)(2,1)} %collective-permute-done.20), channel_id=1, source_target_pairs={{0,2},{2,0},{4,6},{6,4},{1,3},{3,1},{5,7},{7,5},{8,10},{10,8},{12,... | collective-permute-start | bytes 2359304 | tf_op jit(solution)/shard_map/ppermute | solution.py:143
  738.0 16.6 %collective-permute-start.26 = (bf16[768,512]{1,0:T(8,128)(2,1)}, bf16[768,512]{1,0:T(8,128)(2,1)S(1)}, u32[]{:S(2)}, u32[]{:S(2)}) collective-permute-start(bf16[768,512]{1,0:T(8,128)(2,1)} %collective-permute-done.22), channel_id=1, source_target_pairs={{0,2},{2,0},{4,6},{6,4},{1,3},{3,1},{5,7},{7,5},{8,10},{10,8},{12,... | collective-permute-start | bytes 2359304 | tf_op jit(solution)/shard_map/ppermute | solution.py:143
  761.8 3.4 copy-start.5
